TPU v7x, 32 devices: a whole 2x2x4 slice. The times are simulated.
32 devices in a mesh: fsdp: 16 (over z, y, core), tp: 2 (over x).
Axes of the slice: x: 2, y: 2, z: 4, core: 2. Of those that a mesh axis runs over, the one named last changes fastest.
Arguments:
- tokens: bfloat16 [512, 8192], P('tp', 'fsdp'), may hold values from -6 to 6
- gate_blocks: bfloat16 [256, 22, 128, 128], P(('fsdp', 'tp')), may hold values from -0.109375 to 0.109375
- up_blocks: bfloat16 [256, 22, 128, 128], P(('fsdp', 'tp')), may hold values from -0.109375 to 0.109375
- down_blocks: bfloat16 [256, 22, 128, 128], P(('fsdp', 'tp')), may hold values from -0.0546875 to 0.0546875
- gate_index: int32 [256, 22], P('fsdp'), may hold values from 0 to 63, as said below
- up_index: int32 [256, 22], P('fsdp'), may hold values from 0 to 63, as said below
- down_index: int32 [256, 22], P('fsdp'), may hold values from 0 to 63, as said below
- gate_count: int32 [256], P('fsdp'), may hold values from 14 to 22
- up_count: int32 [256], P('fsdp'), may hold values from 14 to 22
- down_count: int32 [256], P('fsdp'), may hold values from 14 to 22
Outputs:
- mixed: bfloat16 [512, 8192], P('tp', 'fsdp')
Inputs may be any that keep to these rules, and one draw needn't show every extreme that they name: `gate_index`: in each row the first gate_count entries name the kept row blocks of that block column; the 22 entries of a row are different numbers. `up_index`: in each row the first up_count entries name the kept row blocks of that block column; the 22 entries of a row are different numbers. `down_index`: in each row the first down_count entries name the kept column blocks of that block row; the 22 entries of a row are different numbers.
All inputs are finite; a program needn't handle non-finite values.
Results may differ from a plain program's by a relative error of at most 0.0049.
Values may be sent and summed in bfloat16 or wider, within the bound.
A program may use at most 256 MiB of HBM per device.

v0:
```python
import jax
import jax.numpy as jnp
from jax import lax
from jax.sharding import PartitionSpec as P


def kept_mask(count_part, slot_num):
    return jnp.arange(slot_num, dtype=jnp.int32)[None, :] < count_part[:, None]


def scatter_rows(partial_out):
    return lax.psum_scatter(partial_out, "fsdp", scatter_dimension=1, tiled=True).astype(
        jnp.bfloat16
    )


def body(
    tokens,
    gate_blocks,
    up_blocks,
    down_blocks,
    gate_index,
    up_index,
    down_index,
    gate_count,
    up_count,
    down_count,
):
    whole = lax.all_gather(tokens, "fsdp", axis=1, tiled=True)
    side_len = gate_blocks.shape[-1]
    row_blocks = whole.shape[1] // side_len
    slot_num = gate_index.shape[1]
    block_ids = jnp.arange(row_blocks, dtype=jnp.int32)

    def project_in(block_set, index_part, count_part):
        col_num = index_part.shape[0]
        live_mask = kept_mask(count_part, slot_num)
        onehot = (
            (index_part[:, :, None] == block_ids[None, None, :]) & live_mask[:, :, None]
        ).astype(jnp.bfloat16)
        panel = jnp.einsum("jki,jkcd->icjd", onehot, block_set, preferred_element_type=jnp.bfloat16)
        panel = panel.reshape(row_blocks * side_len, col_num * side_len)
        return jnp.dot(whole, panel, preferred_element_type=jnp.float32)

    pieces = (
        lax.all_gather(gate_blocks, "tp", axis=0, tiled=True),
        lax.all_gather(up_blocks, "tp", axis=0, tiled=True),
    )
    col_num = pieces[0].shape[0]
    gate_part = project_in(pieces[0], gate_index, gate_count)
    up_part = project_in(pieces[1], up_index, up_count)
    hidden = (jax.nn.silu(gate_part) * up_part).astype(jnp.bfloat16)
    piece = lax.all_gather(down_blocks, "tp", axis=0, tiled=True)
    col_num = piece.shape[0]
    index_part = down_index
    count_part = down_count
    live_mask = kept_mask(count_part, slot_num)
    col_num = piece.shape[0]
    live_mask = kept_mask(count_part, slot_num)
    onehot = ((index_part[:, :, None] == block_ids[None, None, :]) & live_mask[:, :, None]).astype(
        jnp.bfloat16
    )
    panel = jnp.einsum("jki,jkcd->jcid", onehot, piece, preferred_element_type=jnp.bfloat16)
    panel = panel.reshape(col_num * side_len, row_blocks * side_len)
    partial_out = jnp.dot(hidden, panel, preferred_element_type=jnp.float32)
    return scatter_rows(partial_out)


def solution(mesh):
    in_specs = (
        P("tp", "fsdp"),
        P(("fsdp", "tp"), None, None, None),
        P(("fsdp", "tp"), None, None, None),
        P(("fsdp", "tp"), None, None, None),
        P("fsdp", None),
        P("fsdp", None),
        P("fsdp", None),
        P("fsdp"),
        P("fsdp"),
        P("fsdp"),
    )
    out_specs = P("tp", "fsdp")
    return jax.shard_map(body, mesh=mesh, in_specs=in_specs, out_specs=out_specs, check_vma=False)
```

profile of v0, /device:TPU:0, one launch (start us, length us, event | category | flops | bytes accessed | tf_op | source)
XLA Modules:
  0.0 653.1 jit_solution(11383364266053984562)
XLA Ops:
  6.5 0.0 all-gather.5.cloned.1.call-start
  6.6 0.7 all-gather.5.cloned.1.call-update
  7.3 0.0 all-gather.9.cloned.1.call-start
  7.3 0.7 all-gather.9.cloned.1.call-update
  8.0 0.0 all-gather.7.cloned.1.call-start
  8.1 0.7 all-gather.7.cloned.1.call-update
  8.8 0.0 all-gather.11.cloned.1.call-start
  8.8 0.5 all-gather.11.cloned.1.call-update
  9.3 0.0 reduce-scatter.2.cloned.1.call-start
  9.4 0.0 copy-done.3
  9.4 0.1 iota_compare_fusion.5
  9.5 0.0 copy-done.4
  9.5 0.1 iota_compare_fusion.4
  9.5 0.0 copy-done.5
  9.5 0.1 iota_compare_fusion.3
  9.6 143.1 %all-gather.5.cloned.1.call-done = bf16[16,22,128,128]{3,2,1,0:T(8,128)(2,1)} async-done(((bf16[8,22,128,128]{3,2,1,0:T(8,128)(2,1)}), bf16[16,22,128,128]{3,2,1,0:T(8,128)(2,1)}) %all-gather.5.cloned.1.call-update) | async-done | bytes 11534352 | tf_op jit(solution)/shard_map/all_gather | solution.py:46
  152.7 0.0 copy-done
  152.7 21.9 %convolution_bitcast_fusion.1 = bf16[64,128,16,128]{3,0,1,2:T(8,128)(2,1)} fusion(bf16[16,22,128,128]{3,2,1,0:T(8,128)(2,1)} %all-gather.5.cloned.1.call-done, s32[16,22]{1,0:T(8,128)S(1)} %copy-done, pred[16,22]{1,0:T(8,128)(4,1)S(1)} %iota_compare_fusion.5), kind=kOutput, calls=%fused_computation.10 | convolution fusion | flops 738242560 | bytes 45090528 | tf_op jit(solution)/shard_map/jki,jkcd->icjd/dot_general | solution.py:41
  174.5 29.7 %copy.20 = bf16[64,128,16,128]{3,2,1,0:T(8,128)(2,1)} copy(bf16[64,128,16,128]{3,0,1,2:T(8,128)(2,1)} %convolution_bitcast_fusion.1) | data formatting | bytes 67108864 | tf_op jit(solution)/shard_map/jki,jkcd->icjd/transpose | solution.py:41
  204.3 91.0 %all-gather.9.cloned.1.call-done = bf16[16,22,128,128]{3,2,1,0:T(8,128)(2,1)} async-done(((bf16[8,22,128,128]{3,2,1,0:T(8,128)(2,1)}), bf16[16,22,128,128]{3,2,1,0:T(8,128)(2,1)}) %all-gather.9.cloned.1.call-update) | async-done | bytes 11534352 | tf_op jit(solution)/shard_map/all_gather | solution.py:47
  295.3 18.8 %convolution_bitcast_fusion = bf16[64,128,16,128]{3,0,1,2:T(8,128)(2,1)} fusion(bf16[16,22,128,128]{3,2,1,0:T(8,128)(2,1)} %all-gather.9.cloned.1.call-done, s32[16,22]{1,0:T(8,128)S(1)} %copy-done.1, pred[16,22]{1,0:T(8,128)(4,1)S(1)} %iota_compare_fusion.4), kind=kOutput, calls=%fused_computation.9 | convolution fusion | flops 738242560 | bytes 45090528 | tf_op jit(solution)/shard_map/jki,jkcd->icjd/dot_general | solution.py:41
  314.1 29.5 %copy.22 = bf16[64,128,16,128]{3,2,1,0:T(8,128)(2,1)} copy(bf16[64,128,16,128]{3,0,1,2:T(8,128)(2,1)} %convolution_bitcast_fusion) | data formatting | bytes 67108864 | tf_op jit(solution)/shard_map/jki,jkcd->icjd/transpose | solution.py:41
  343.6 7.1 %all-gather.7.cloned.1.call-done = bf16[256,8192]{1,0:T(8,128)(2,1)} async-done(((bf16[256,512]{1,0:T(8,128)(2,1)}), bf16[256,8192]{1,0:T(8,128)(2,1)}) %all-gather.7.cloned.1.call-update) | async-done | bytes 4194320 | tf_op jit(solution)/shard_map/all_gather | solution.py:29
  350.7 28.7 %fusion.13 = f32[256,2048]{0,1:T(8,128)S(1)} fusion(bf16[256,8192]{1,0:T(8,128)(2,1)} %all-gather.7.cloned.1.call-done, bf16[1024,8,16,128]{3,2,1,0:T(8,128)(2,1)} %bitcast.55), kind=kOutput, calls=%fused_computation.15 | convolution fusion | flops 8589934592 | bytes 39845888 | tf_op jit(solution)/shard_map/dot_general | solution.py:43
  379.4 0.0 copy-start.2
  379.4 26.4 %fusion.22 = bf16[256,2048]{0,1:T(8,128)(2,1)S(1)} fusion(bf16[256,8192]{1,0:T(8,128)(2,1)} %all-gather.7.cloned.1.call-done, bf16[1024,8,16,128]{3,2,1,0:T(8,128)(2,1)} %bitcast.56, f32[256,2048]{0,1:T(8,128)S(1)} %fusion.13), kind=kOutput, calls=%fused_computation.18 | convolution fusion | flops 8593080320 | bytes 40894464 | tf_op jit(solution)/shard_map/dot_general | solution.py:43
  405.9 85.5 %all-gather.11.cloned.1.call-done = bf16[16,22,128,128]{3,2,1,0:T(8,128)(2,1)} async-done(((bf16[8,22,128,128]{3,2,1,0:T(8,128)(2,1)}), bf16[16,22,128,128]{3,2,1,0:T(8,128)(2,1)}) %all-gather.11.cloned.1.call-update) | async-done | bytes 11534352 | tf_op jit(solution)/shard_map/all_gather | solution.py:53
  491.4 18.8 %fusion.9 = bf16[16,64,128,128]{3,1,2,0:T(8,128)(2,1)} fusion(bf16[16,22,128,128]{3,2,1,0:T(8,128)(2,1)} %all-gather.11.cloned.1.call-done, s32[16,22]{1,0:T(8,128)S(1)} %copy-done.2, pred[16,22]{1,0:T(8,128)(4,1)S(1)} %iota_compare_fusion.3), kind=kOutput, calls=%fused_computation.11 | convolution fusion | flops 738242560 | bytes 45090528 | tf_op jit(solution)/shard_map/jki,jkcd->jcid/dot_general | solution.py:63
  510.1 29.2 %fusion = f32[256,8192]{1,0:T(8,128)} fusion(bf16[256,2048]{0,1:T(8,128)(2,1)S(1)} %fusion.22, bf16[256,8,64,128]{3,2,1,0:T(8,128)(2,1)} %bitcast.54), kind=kOutput, calls=%fused_computation | convolution fusion | flops 8589934592 | bytes 42991616 | tf_op jit(solution)/shard_map/dot_general | solution.py:65
  539.3 0.0 reduce-scatter.2.cloned.1.call-update
  539.3 105.0 %reduce-scatter.2.cloned.1.call-done = f32[256,512]{1,0:T(8,128)} async-done(((f32[256,8192]{1,0:T(8,128)}), f32[256,512]{1,0:T(8,128)}) %reduce-scatter.2.cloned.1.call-update) | async-done | bytes 524304 | tf_op jit(solution)/shard_map/reduce_scatter | solution.py:12
  644.4 1.8 convert_element_type.10
  (7 shorter events, 0.0 us)
Async XLA Ops:
  6.5 2.8 copy-start.3
  6.5 2.9 copy-start.4
  6.5 3.0 copy-start.5
  6.5 146.1 %copy-start = (s32[16,22]{1,0:T(8,128)S(1)}, s32[16,22]{1,0:T(8,128)}, u32[]{:S(2)}) copy-start(s32[16,22]{1,0:T(8,128)} %param.14) | copy-start | bytes 4228
  6.5 146.1 %all-gather.5.cloned.1.call-start = ((), (), s32[]{:S(2)}) async-start(), calls=%async_computation.1 | async-start | bytes 17301504 | tf_op jit(solution)/shard_map/all_gather | solution.py:46
  7.3 288.0 %all-gather.9.cloned.1.call-start = ((), (), s32[]{:S(2)}) async-start(), calls=%async_computation.3 | async-start | bytes 17301504 | tf_op jit(solution)/shard_map/all_gather | solution.py:47
  8.0 342.7 %all-gather.7.cloned.1.call-start = ((), (), s32[]{:S(2)}) async-start(), calls=%async_computation.2 | async-start | bytes 4456448 | tf_op jit(solution)/shard_map/all_gather | solution.py:29
  8.8 482.6 %all-gather.11.cloned.1.call-start = ((), (), s32[]{:S(2)}) async-start(), calls=%async_computation.4 | async-start | bytes 17301504 | tf_op jit(solution)/shard_map/all_gather | solution.py:53
  9.3 635.0 %reduce-scatter.2.cloned.1.call-start = ((), (), s32[]{:S(2)}) async-start(), calls=%async_computation.5 | async-start | bytes 8912896 | tf_op jit(solution)/shard_map/reduce_scatter | solution.py:12
  174.5 120.8 %copy-start.1 = (s32[16,22]{1,0:T(8,128)S(1)}, s32[16,22]{1,0:T(8,128)}, u32[]{:S(2)}) copy-start(s32[16,22]{1,0:T(8,128)} %param.15) | copy-start | bytes 4228
  379.4 111.9 %copy-start.2 = (s32[16,22]{1,0:T(8,128)S(1)}, s32[16,22]{1,0:T(8,128)}, u32[]{:S(2)}) copy-start(s32[16,22]{1,0:T(8,128)} %param.16) | copy-start | bytes 4228
Sparse Core Ops, SparseCore 0:
  8.9 143.6 all-gather.4
  154.2 141.0 all-gather.8
  297.4 53.2 all-gather.6
  352.1 139.1 all-gather.10
  539.5 104.8 reduce-scatter.1
where the time goes:
time: 661 us; the launch traced here: 653 us
  waiting for transfers between devices  434 us (66%)
  matrix products  144 us (22%)
  local copies, waits for them, and re-layouts  59.3 us (9%)
  between operations  13.6 us (2%)
    all_gather x1, waiting for transfers between devices, body(): lax.all_gather(gate_blocks, 'tp', axis=0, tiled=True)  143 us
    reduce_scatter x1, waiting for transfers between devices, scatter_rows(): lax.psum_scatter(partial_out, 'fsdp', scatter_dimension=1, tiled=True)  105 us
    all_gather x1, waiting for transfers between devices, body(): lax.all_gather(up_blocks, 'tp', axis=0, tiled=True)  91 us
    all_gather x1, waiting for transfers between devices, body(): piece = lax.all_gather(down_blocks, 'tp', axis=0, tiled=True)  85.5 us
    transpose x2, local copies, waits for them, and re-layouts, project_in(): jnp.einsum('jki,jkcd->icjd', onehot, block_set, preferred_element_type=jn...  59.3 us
    dot_general x2, matrix products, project_in(): return jnp.dot(whole, panel, preferred_element_type=jnp.float32)  55.1 us
    dot_general x2, matrix products, project_in(): jnp.einsum('jki,jkcd->icjd', onehot, block_set, preferred_element_type=jn...  40.7 us
    dot_general x1, matrix products, body(): partial_out = jnp.dot(hidden, panel, preferred_element_type=jnp.float32)  29.2 us
  transfers between devices with their start and end apart: 5, of which 5 were waited for; matrix products, arithmetic and copies ran while one was open for 24% of the time, Pallas kernels for 0%

commit v1 on v0

v1 whole, which is shorter than its diff:
```python
import functools

import jax
import jax.numpy as jnp
from jax import lax
from jax.experimental import pallas as pl
from jax.experimental.pallas import tpu as pltpu
from jax.sharding import PartitionSpec as P

MESH = pl.DeviceIdType.MESH
VMEM_BYTES = 56 * 1024 * 1024


def kept_mask(count_part, slot_num):
    return jnp.arange(slot_num, dtype=jnp.int32)[None, :] < count_part[:, None]


def general_body(
    tokens,
    gate_blocks,
    up_blocks,
    down_blocks,
    gate_index,
    up_index,
    down_index,
    gate_count,
    up_count,
    down_count,
):
    whole = lax.all_gather(tokens, "fsdp", axis=1, tiled=True)
    side_len = gate_blocks.shape[-1]
    row_blocks = whole.shape[1] // side_len
    slot_num = gate_index.shape[1]
    block_ids = jnp.arange(row_blocks, dtype=jnp.int32)

    def onehot_of(index_part, count_part):
        live_mask = kept_mask(count_part, slot_num)
        return (
            (index_part[:, :, None] == block_ids[None, None, :]) & live_mask[:, :, None]
        ).astype(jnp.bfloat16)

    def project_in(block_set, index_part, count_part):
        onehot = onehot_of(index_part, count_part)
        panel = jnp.einsum("jki,jkcd->icjd", onehot, block_set, preferred_element_type=jnp.bfloat16)
        panel = panel.reshape(row_blocks * side_len, index_part.shape[0] * side_len)
        return jnp.dot(whole, panel, preferred_element_type=jnp.float32)

    gate_part = project_in(
        lax.all_gather(gate_blocks, "tp", axis=0, tiled=True), gate_index, gate_count
    )
    up_part = project_in(lax.all_gather(up_blocks, "tp", axis=0, tiled=True), up_index, up_count)
    hidden = (jax.nn.silu(gate_part) * up_part).astype(jnp.bfloat16)
    piece = lax.all_gather(down_blocks, "tp", axis=0, tiled=True)
    panel = jnp.einsum(
        "jki,jkcd->jcid",
        onehot_of(down_index, down_count),
        piece,
        preferred_element_type=jnp.bfloat16,
    )
    panel = panel.reshape(piece.shape[0] * side_len, row_blocks * side_len)
    partial_out = jnp.dot(hidden, panel, preferred_element_type=jnp.float32)
    return lax.psum_scatter(partial_out, "fsdp", scatter_dimension=1, tiled=True).astype(
        jnp.bfloat16
    )


class Place:
    def __init__(self, depth):
        fs = lax.axis_index("fsdp")
        self.depth = depth
        self.fs = fs
        self.x = lax.axis_index("tp")
        self.c = fs % 2
        self.y = (fs // 2) % 2
        self.z = fs // 4

    def spot(self, s, z, c):
        across_a, across_b = s % 2, s // 2
        dx = across_b * (1 - c) + across_a * c
        dy = across_a * (1 - c) + across_b * c
        return (z * 2 + (self.y + dy) % 2) * 2 + c, (self.x + dx) % 2

    def behind(self, d):
        return (self.z + self.depth - d) % self.depth

    def ahead(self, d):
        return (self.z + d) % self.depth

    def device(self, s):
        f, t = self.spot(s, self.z, self.c)
        return {"fsdp": f, "tp": t}

    def other_core(self):
        return {"fsdp": self.fs + 1 - 2 * self.c, "tp": self.x}

    def along_z(self, d):
        return {"fsdp": (self.ahead(d) * 2 + self.y) * 2 + self.c, "tp": self.x}


def greet(place):
    barrier = pltpu.get_barrier_semaphore()
    partners = [place.device(1), place.device(2), place.other_core()]
    partners += [place.along_z(d) for d in range(1, place.depth)]
    for partner in partners:
        pl.semaphore_signal(barrier, inc=1, device_id=partner, device_id_type=MESH)
    pl.semaphore_wait(barrier, len(partners))


def remote(src, dst, send_sem, recv_sem, device):
    return pltpu.make_async_remote_copy(
        src_ref=src,
        dst_ref=dst,
        send_sem=send_sem,
        recv_sem=recv_sem,
        device_id=device,
        device_id_type=MESH,
    )


def in_kernel(
    depth,
    slot_of,
    tokens,
    gate_hbm,
    up_hbm,
    hidden,
    tok,
    weights,
    acc,
    load_sem,
    z_send,
    a_send,
    b_send,
    c_send,
    plane_recv,
    core_recv,
):
    place = Place(depth)
    cols, slots = gate_hbm.shape[0], gate_hbm.shape[1]
    side = gate_hbm.shape[2]
    rows = tokens.shape[0]
    group = tokens.shape[1] // side
    pairs = cols // 2

    loads = [
        pltpu.make_async_copy(src, weights.at[m, :, pl.ds(0, slots)], load_sem.at[m])
        for m, src in enumerate((gate_hbm, up_hbm))
    ]
    for load in loads:
        load.start()
    tok[place.fs, place.x] = tokens[...]
    greet(place)

    def shard(s, d):
        f, t = place.spot(s, place.behind(d), place.c)
        return tok.at[f, t]

    def to_a(d):
        return remote(shard(0, d), shard(0, d), a_send.at[d], plane_recv.at[1, d], place.device(1))

    def to_b(s, d):
        return remote(
            shard(s, d), shard(s, d), b_send.at[s, d], plane_recv.at[s + 2, d], place.device(2)
        )

    def to_core(s, d):
        return remote(
            shard(s, d), shard(s, d), c_send.at[s, d], core_recv.at[s, d], place.other_core()
        )

    def to_z(d):
        return remote(
            shard(0, 0), shard(0, 0), z_send.at[d], plane_recv.at[0, d], place.along_z(d)
        )

    def arrived(s, d):
        ref = shard(s, d)
        remote(ref, ref, c_send.at[s, d], plane_recv.at[s, d], place.other_core()).wait_recv()

    def arrived_core(s, d):
        f, t = place.spot(s, place.behind(d), 1 - place.c)
        ref = tok.at[f, t]
        remote(ref, ref, c_send.at[s, d], core_recv.at[s, d], place.other_core()).wait_recv()

    to_a(0).start()
    to_b(0, 0).start()
    for d in range(1, depth):
        to_z(d).start()
    to_core(0, 0).start()

    weights[:, :, slots] = jnp.zeros((2, cols, side, side), weights.dtype)
    acc[...] = jnp.zeros_like(acc)
    for load in loads:
        load.wait()

    def multiply(d, dy, c):
        f = (place.behind(d) * 2 + (place.y + dy) % 2) * 2 + c
        left = tok[f].reshape(2 * rows, group * side)

        def pair(n, carry):
            for m in range(2):
                panel = jnp.concatenate(
                    [
                        jnp.concatenate(
                            [
                                weights[m, 2 * n + e, slot_of[m * cols + 2 * n + e, f * group + i]]
                                for e in range(2)
                            ],
                            axis=1,
                        )
                        for i in range(group)
                    ],
                    axis=0,
                )
                acc[m, n] += jnp.dot(left, panel, preferred_element_type=jnp.float32)
            return carry

        lax.fori_loop(0, pairs, pair, 0)

    def stage(d, carry):
        @pl.when(d + 1 < depth)
        def _():
            arrived(0, d + 1)
            to_a(d + 1).start()
            to_b(0, d + 1).start()
            to_core(0, d + 1).start()

        arrived(1, d)
        to_b(1, d).start()
        to_core(1, d).start()
        arrived(2, d)
        to_core(2, d).start()
        multiply(d, 0, place.c)
        arrived(3, d)
        to_core(3, d).start()
        for s in range(3):
            arrived_core(s, d)
        multiply(d, 0, 1 - place.c)
        multiply(d, 1, place.c)
        arrived_core(3, d)
        multiply(d, 1, 1 - place.c)
        return carry

    lax.fori_loop(0, depth, stage, 0)

    for n in range(pairs):
        gate = acc[0, n]
        up = acc[1, n]
        out = (gate / (1.0 + jnp.exp(-gate)) * up).astype(hidden.dtype)
        hidden[:, :, n * 2 * side : (n + 1) * 2 * side] = out.reshape(2, rows, 2 * side)

    for d in range(depth):
        if d:
            to_z(d).wait_send()
        to_a(d).wait_send()
        for s in range(2):
            to_b(s, d).wait_send()
        for s in range(4):
            to_core(s, d).wait_send()


def out_kernel(
    depth,
    slot_of,
    hidden,
    down_hbm,
    mixed,
    weights,
    total,
    core_out,
    core_in,
    b_out,
    b_in,
    a_out,
    a_in,
    z_out,
    z_in,
    load_sem,
    c_send,
    c_recv,
    b_send,
    b_recv,
    a_send,
    a_recv,
    z_send,
    z_recv,
):
    place = Place(depth)
    cols, slots, side = down_hbm.shape[0], down_hbm.shape[1], down_hbm.shape[2]
    group = mixed.shape[1] // side
    pairs = group // 2

    load = pltpu.make_async_copy(down_hbm, weights.at[:, pl.ds(0, slots)], load_sem)
    load.start()
    weights[:, slots] = jnp.zeros((cols, side, side), weights.dtype)
    greet(place)
    load.wait()

    def share(f, t, store):
        left = hidden[t]
        for n in range(pairs):
            panel = jnp.concatenate(
                [
                    jnp.concatenate(
                        [weights[j, slot_of[j, f * group + 2 * n + e]] for e in range(2)], axis=1
                    )
                    for j in range(cols)
                ],
                axis=0,
            )
            store(
                slice(n * 2 * side, (n + 1) * 2 * side),
                jnp.dot(left, panel, preferred_element_type=jnp.float32),
            )

    def to_core(s, d):
        return remote(
            core_out.at[s, d],
            core_in.at[s, d],
            c_send.at[s, d],
            c_recv.at[s, d],
            place.other_core(),
        )

    def to_b(s, d):
        return remote(
            b_out.at[s, d], b_in.at[s, d], b_send.at[s, d], b_recv.at[s, d], place.device(2)
        )

    def to_a(d):
        return remote(a_out.at[d], a_in.at[d], a_send.at[d], a_recv.at[d], place.device(1))

    def to_z(d):
        return remote(z_out.at[d], z_in.at[d], z_send.at[d], z_recv.at[d], place.along_z(d))

    for s in (3, 2, 1, 0):

        def step(k, carry, s=s):
            d = (k + 1) % depth
            f, t = place.spot(s, place.ahead(d), 1 - place.c)

            def store_out(where, value):
                core_out[s, d, :, where] = value.astype(core_out.dtype)

            share(f, t, store_out)
            to_core(s, d).start()
            f, t = place.spot(s, place.ahead(d), place.c)

            def store_own(where, value):
                total[s, d, :, where] = value

            share(f, t, store_own)
            to_core(s, d).wait_recv()
            value = total[s, d] + core_in[s, d].astype(jnp.float32)
            if s >= 2:
                b_out[s - 2, d] = value.astype(b_out.dtype)
                to_b(s - 2, d).start()
            else:
                total[s, d] = value
            return carry

        lax.fori_loop(0, depth, step, 0)

    def cross_a(k, carry):
        d = (k + 1) % depth
        to_b(1, d).wait_recv()
        a_out[d] = (total[1, d] + b_in[1, d].astype(jnp.float32)).astype(a_out.dtype)
        to_a(d).start()
        return carry

    lax.fori_loop(0, depth, cross_a, 0)

    def cross_z(k, carry):
        d = (k + 1) % depth
        to_b(0, d).wait_recv()
        to_a(d).wait_recv()
        value = total[0, d] + b_in[0, d].astype(jnp.float32) + a_in[d].astype(jnp.float32)

        @pl.when(d > 0)
        def _():
            z_out[d] = value.astype(z_out.dtype)
            to_z(d).start()

        @pl.when(d == 0)
        def _():
            total[0, d] = value

        return carry

    lax.fori_loop(0, depth, cross_z, 0)
    value = total[0, 0]
    for d in range(1, depth):
        to_z(d).wait_recv()
        value = value + z_in[d].astype(jnp.float32)
    mixed[...] = value.astype(mixed.dtype)

    for d in range(depth):
        if d:
            to_z(d).wait_send()
        to_a(d).wait_send()
        for s in range(2):
            to_b(s, d).wait_send()
        for s in range(4):
            to_core(s, d).wait_send()


def plane_body(
    depth,
    tokens,
    gate_blocks,
    up_blocks,
    down_blocks,
    gate_index,
    up_index,
    down_index,
    gate_count,
    up_count,
    down_count,
):
    rows, feats = tokens.shape
    cols, slots, side = gate_blocks.shape[:3]
    fsdp = 4 * depth
    row_blocks = fsdp * feats // side
    bf16 = tokens.dtype

    first = lax.axis_index("tp") * cols
    index = jnp.stack([gate_index, up_index, down_index])
    count = jnp.stack([gate_count, up_count, down_count])
    index = lax.dynamic_slice_in_dim(index, first, cols, 1)
    count = lax.dynamic_slice_in_dim(count, first, cols, 1)
    slot_ids = jnp.arange(slots, dtype=jnp.int32)[None, None, :, None]
    block_ids = jnp.arange(row_blocks, dtype=jnp.int32)[None, None, None, :]
    hit = (index[..., None] == block_ids) & (slot_ids < count[:, :, None, None])
    slot_of = jnp.min(jnp.where(hit, slot_ids, slots), axis=2)

    vmem = pl.BlockSpec(memory_space=pltpu.VMEM)
    smem = pl.BlockSpec(memory_space=pltpu.SMEM)
    anywhere = pl.BlockSpec(memory_space=pl.ANY)
    dma = pltpu.SemaphoreType.DMA

    hidden = pl.pallas_call(
        functools.partial(in_kernel, depth),
        out_shape=jax.ShapeDtypeStruct((2, rows, cols * side), bf16),
        in_specs=[smem, vmem, anywhere, anywhere],
        out_specs=vmem,
        scratch_shapes=[
            pltpu.VMEM((fsdp, 2, rows, feats), bf16),
            pltpu.VMEM((2, cols, slots + 1, side, side), bf16),
            pltpu.VMEM((2, cols // 2, 2 * rows, 2 * side), jnp.float32),
            dma((2,)),
            dma((depth,)),
            dma((depth,)),
            dma((2, depth)),
            dma((4, depth)),
            dma((4, depth)),
            dma((4, depth)),
        ],
        compiler_params=pltpu.CompilerParams(
            collective_id=0, has_side_effects=True, vmem_limit_bytes=VMEM_BYTES
        ),
    )(slot_of[:2].reshape(2 * cols, row_blocks), tokens, gate_blocks, up_blocks)

    return pl.pallas_call(
        functools.partial(out_kernel, depth),
        out_shape=jax.ShapeDtypeStruct((rows, feats), bf16),
        in_specs=[smem, vmem, anywhere],
        out_specs=vmem,
        scratch_shapes=[
            pltpu.VMEM((cols, slots + 1, side, side), bf16),
            pltpu.VMEM((4, depth, rows, feats), jnp.float32),
            pltpu.VMEM((4, depth, rows, feats), bf16),
            pltpu.VMEM((4, depth, rows, feats), bf16),
            pltpu.VMEM((2, depth, rows, feats), bf16),
            pltpu.VMEM((2, depth, rows, feats), bf16),
            pltpu.VMEM((depth, rows, feats), bf16),
            pltpu.VMEM((depth, rows, feats), bf16),
            pltpu.VMEM((depth, rows, feats), bf16),
            pltpu.VMEM((depth, rows, feats), bf16),
            dma(()),
            dma((4, depth)),
            dma((4, depth)),
            dma((2, depth)),
            dma((2, depth)),
            dma((depth,)),
            dma((depth,)),
            dma((depth,)),
            dma((depth,)),
        ],
        compiler_params=pltpu.CompilerParams(
            collective_id=1, has_side_effects=True, vmem_limit_bytes=VMEM_BYTES
        ),
    )(slot_of[2], hidden, down_blocks)


def solution(mesh):
    fsdp, tp = mesh.shape["fsdp"], mesh.shape["tp"]
    if tp == 2 and fsdp % 4 == 0:
        body = functools.partial(plane_body, fsdp // 4)
    else:
        body = general_body
    in_specs = (
        P("tp", "fsdp"),
        P(("fsdp", "tp"), None, None, None),
        P(("fsdp", "tp"), None, None, None),
        P(("fsdp", "tp"), None, None, None),
        P("fsdp", None),
        P("fsdp", None),
        P("fsdp", None),
        P("fsdp"),
        P("fsdp"),
        P("fsdp"),
    )
    out_specs = P("tp", "fsdp")
    return jax.shard_map(body, mesh=mesh, in_specs=in_specs, out_specs=out_specs, check_vma=False)
```

time: 661 us -> 146 us (0.22)
  the two profiles are of different devices: /device:TPU:0 before, /device:TPU:9 now
where the time goes in v1:
time: 146 us
  Pallas kernels  141 us (97%)
  local copies, waits for them, and re-layouts  3.03 us (2%)
  other arithmetic  1.65 us (1%)
    pallas_call x1, Pallas kernels, plane_body(): pl.pallas_call(functools.partial(out_kernel, depth), out_shape=jax.ShapeD...  71.2 us
    pallas_call x1, Pallas kernels, plane_body(): pl.pallas_call(functools.partial(in_kernel, depth), out_shape=jax.ShapeDt...  69.8 us

profile of v1, /device:TPU:9, one launch (start us, length us, event | category | flops | bytes accessed | tf_op | source)
XLA Modules:
  0.0 145.7 jit_solution(12361339333961363070)
XLA Ops:
  0.0 0.7 pad_add_fusion
  0.7 0.1 constant_dynamic-slice_fusion
  0.8 0.7 fusion.2
  1.5 0.1 copy.11
  1.6 0.2 select_reduce_fusion
  1.8 0.6 slice_bitcast_fusion.1.slot_of
  2.4 0.6 slice_bitcast_fusion.slot_of
  3.0 69.8 %shard_map.100.hidden = bf16[2,256,1024]{2,1,0:T(8,128)(2,1)} custom-call(s32[16,64]{1,0:T(8,128)} %slice_bitcast_fusion.slot_of, bf16[256,512]{1,0:T(8,128)(2,1)} %tokens.1, bf16[8,22,128,128]{3,2,1,0:T(8,128)(2,1)} %gate_hbm.1, bf16[8,22,128,128]{3,2,1,0:T(8,128)(2,1)} %up_hbm.1), custom_call_target="tpu_custom_call" | custom-call | tf_op jit(solution)/shard_map/pallas_call | solution.py:441
  72.9 71.2 %shard_map.101 = bf16[256,512]{1,0:T(8,128)(2,1)} custom-call(s32[8,64]{1,0:T(8,128)} %slice_bitcast_fusion.1.slot_of, bf16[2,256,1024]{2,1,0:T(8,128)(2,1)} %shard_map.100.hidden, bf16[8,22,128,128]{3,2,1,0:T(8,128)(2,1)} %down_hbm.1), custom_call_target="tpu_custom_call" | custom-call | tf_op jit(solution)/shard_map/pallas_call | solution.py:463
  144.1 1.7 %copy.13 = bf16[256,512]{1,0:T(8,128)(2,1)} copy(bf16[256,512]{1,0:T(8,128)(2,1)} %shard_map.101) | data formatting | bytes 524288
  (1 shorter events, 0.0 us)

commit v2 on v1

--- a/solution.py
+++ b/solution.py
@@ -80,8 +80,13 @@
         dy = across_a * (1 - c) + across_b * c
         return (z * 2 + (self.y + dy) % 2) * 2 + c, (self.x + dx) % 2
 
-    def behind(self, d):
-        return (self.z + self.depth - d) % self.depth
+    def order(self, j):
+        below, above = self.z, self.depth - 1 - self.z
+        near = jnp.minimum(below, above)
+        far = j - near
+        one_side = jnp.where(below > above, self.z - far, self.z + far)
+        both = jnp.where(j % 2 == 1, self.z - (j + 1) // 2, self.z + j // 2)
+        return jnp.where(j > 2 * near, one_side, both)
 
     def ahead(self, d):
         return (self.z + d) % self.depth
@@ -93,8 +98,11 @@
     def other_core(self):
         return {"fsdp": self.fs + 1 - 2 * self.c, "tp": self.x}
 
+    def at_z(self, z):
+        return {"fsdp": (z * 2 + self.y) * 2 + self.c, "tp": self.x}
+
     def along_z(self, d):
-        return {"fsdp": (self.ahead(d) * 2 + self.y) * 2 + self.c, "tp": self.x}
+        return self.at_z(self.ahead(d))
 
 
 def greet(place):
@@ -151,50 +159,59 @@
     tok[place.fs, place.x] = tokens[...]
     greet(place)
 
-    def shard(s, d):
-        f, t = place.spot(s, place.behind(d), place.c)
+    def shard(s, z, c):
+        f, t = place.spot(s, z, c)
         return tok.at[f, t]
 
-    def to_a(d):
-        return remote(shard(0, d), shard(0, d), a_send.at[d], plane_recv.at[1, d], place.device(1))
-
-    def to_b(s, d):
-        return remote(
-            shard(s, d), shard(s, d), b_send.at[s, d], plane_recv.at[s + 2, d], place.device(2)
-        )
-
-    def to_core(s, d):
-        return remote(
-            shard(s, d), shard(s, d), c_send.at[s, d], core_recv.at[s, d], place.other_core()
-        )
-
-    def to_z(d):
-        return remote(
-            shard(0, 0), shard(0, 0), z_send.at[d], plane_recv.at[0, d], place.along_z(d)
-        )
-
-    def arrived(s, d):
-        ref = shard(s, d)
-        remote(ref, ref, c_send.at[s, d], plane_recv.at[s, d], place.other_core()).wait_recv()
-
-    def arrived_core(s, d):
-        f, t = place.spot(s, place.behind(d), 1 - place.c)
-        ref = tok.at[f, t]
-        remote(ref, ref, c_send.at[s, d], core_recv.at[s, d], place.other_core()).wait_recv()
-
-    to_a(0).start()
-    to_b(0, 0).start()
-    for d in range(1, depth):
-        to_z(d).start()
-    to_core(0, 0).start()
+    def to_a(z):
+        ref = shard(0, z, place.c)
+        return remote(ref, ref, a_send.at[z], plane_recv.at[1, z], place.device(1))
+
+    def to_b(s, z):
+        ref = shard(s, z, place.c)
+        return remote(ref, ref, b_send.at[s, z], plane_recv.at[s + 2, z], place.device(2))
+
+    def to_core(s, z):
+        ref = shard(s, z, place.c)
+        return remote(ref, ref, c_send.at[s, z], core_recv.at[s, z], place.other_core())
+
+    def to_z(up, z):
+        ref = shard(0, z, place.c)
+        device = place.at_z(place.z + 2 * up - 1)
+        return remote(ref, ref, z_send.at[up, z], plane_recv.at[0, z], device)
+
+    def arrived(s, z):
+        ref = shard(s, z, place.c)
+        remote(ref, ref, c_send.at[s, z], plane_recv.at[s, z], place.other_core()).wait_recv()
+
+    def arrived_core(s, z):
+        ref = shard(s, z, 1 - place.c)
+        remote(ref, ref, c_send.at[s, z], core_recv.at[s, z], place.other_core()).wait_recv()
+
+    def each_relay(z, act):
+        pl.when((z <= place.z) & (place.z < depth - 1))(lambda: act(to_z(1, z)))
+        pl.when((z >= place.z) & (place.z > 0))(lambda: act(to_z(0, z)))
+
+    def begin(z):
+        each_relay(z, lambda copy: copy.start())
+        to_a(z).start()
+        to_b(0, z).start()
+        to_core(0, z).start()
+
+    def take(j):
+        z = place.order(j)
+        arrived(0, z)
+        begin(z)
+
+    begin(place.z)
 
     weights[:, :, slots] = jnp.zeros((2, cols, side, side), weights.dtype)
     acc[...] = jnp.zeros_like(acc)
     for load in loads:
         load.wait()
 
-    def multiply(d, dy, c):
-        f = (place.behind(d) * 2 + (place.y + dy) % 2) * 2 + c
+    def multiply(z, dy, c):
+        f = (z * 2 + (place.y + dy) % 2) * 2 + c
         left = tok[f].reshape(2 * rows, group * side)
 
         def pair(n, carry):
@@ -217,31 +234,50 @@
 
         lax.fori_loop(0, pairs, pair, 0)
 
-    def stage(d, carry):
-        @pl.when(d + 1 < depth)
-        def _():
-            arrived(0, d + 1)
-            to_a(d + 1).start()
-            to_b(0, d + 1).start()
-            to_core(0, d + 1).start()
-
-        arrived(1, d)
-        to_b(1, d).start()
-        to_core(1, d).start()
-        arrived(2, d)
-        to_core(2, d).start()
-        multiply(d, 0, place.c)
-        arrived(3, d)
-        to_core(3, d).start()
-        for s in range(3):
-            arrived_core(s, d)
-        multiply(d, 0, 1 - place.c)
-        multiply(d, 1, place.c)
-        arrived_core(3, d)
-        multiply(d, 1, 1 - place.c)
+    def stage(j, carry):
+        last = place.order(j - 1)
+
+        @pl.when(j + 1 < depth)
+        def _():
+            take(j + 1)
+
+        @pl.when(j < depth)
+        def _():
+            z = place.order(j)
+            arrived(1, z)
+            to_b(1, z).start()
+            to_core(1, z).start()
+
+        @pl.when(j > 0)
+        def _():
+            multiply(last, 0, place.c)
+
+        @pl.when(j < depth)
+        def _():
+            z = place.order(j)
+            arrived(2, z)
+            to_core(2, z).start()
+
+        @pl.when(j > 0)
+        def _():
+            multiply(last, 1, place.c)
+
+        @pl.when(j < depth)
+        def _():
+            z = place.order(j)
+            arrived(3, z)
+            to_core(3, z).start()
+
+        @pl.when(j > 0)
+        def _():
+            for s in range(4):
+                arrived_core(s, last)
+            multiply(last, 0, 1 - place.c)
+            multiply(last, 1, 1 - place.c)
+
         return carry
 
-    lax.fori_loop(0, depth, stage, 0)
+    lax.fori_loop(0, depth + 1, stage, 0)
 
     for n in range(pairs):
         gate = acc[0, n]
@@ -249,14 +285,13 @@
         out = (gate / (1.0 + jnp.exp(-gate)) * up).astype(hidden.dtype)
         hidden[:, :, n * 2 * side : (n + 1) * 2 * side] = out.reshape(2, rows, 2 * side)
 
-    for d in range(depth):
-        if d:
-            to_z(d).wait_send()
-        to_a(d).wait_send()
+    for z in range(depth):
+        each_relay(z, lambda copy: copy.wait_send())
+        to_a(z).wait_send()
         for s in range(2):
-            to_b(s, d).wait_send()
+            to_b(s, z).wait_send()
         for s in range(4):
-            to_core(s, d).wait_send()
+            to_core(s, z).wait_send()
 
 
 def out_kernel(
@@ -333,45 +368,37 @@
     def to_z(d):
         return remote(z_out.at[d], z_in.at[d], z_send.at[d], z_recv.at[d], place.along_z(d))
 
-    for s in (3, 2, 1, 0):
-
-        def step(k, carry, s=s):
-            d = (k + 1) % depth
-            f, t = place.spot(s, place.ahead(d), 1 - place.c)
-
-            def store_out(where, value):
-                core_out[s, d, :, where] = value.astype(core_out.dtype)
-
-            share(f, t, store_out)
-            to_core(s, d).start()
-            f, t = place.spot(s, place.ahead(d), place.c)
-
-            def store_own(where, value):
-                total[s, d, :, where] = value
-
-            share(f, t, store_own)
-            to_core(s, d).wait_recv()
-            value = total[s, d] + core_in[s, d].astype(jnp.float32)
-            if s >= 2:
-                b_out[s - 2, d] = value.astype(b_out.dtype)
-                to_b(s - 2, d).start()
-            else:
-                total[s, d] = value
-            return carry
-
-        lax.fori_loop(0, depth, step, 0)
-
-    def cross_a(k, carry):
-        d = (k + 1) % depth
+    def slab(k):
+        return (k + 1) % depth
+
+    def unit(s, d):
+        f, t = place.spot(s, place.ahead(d), 1 - place.c)
+
+        def store_out(where, value):
+            core_out[s, d, :, where] = value.astype(core_out.dtype)
+
+        share(f, t, store_out)
+        to_core(s, d).start()
+        f, t = place.spot(s, place.ahead(d), place.c)
+
+        def store_own(where, value):
+            total[s, d, :, where] = value
+
+        share(f, t, store_own)
+        to_core(s, d).wait_recv()
+        value = total[s, d] + core_in[s, d].astype(jnp.float32)
+        if s >= 2:
+            b_out[s - 2, d] = value.astype(b_out.dtype)
+            to_b(s - 2, d).start()
+        else:
+            total[s, d] = value
+
+    def cross_a(d):
         to_b(1, d).wait_recv()
         a_out[d] = (total[1, d] + b_in[1, d].astype(jnp.float32)).astype(a_out.dtype)
         to_a(d).start()
-        return carry
-
-    lax.fori_loop(0, depth, cross_a, 0)
-
-    def cross_z(k, carry):
-        d = (k + 1) % depth
+
+    def cross_z(d):
         to_b(0, d).wait_recv()
         to_a(d).wait_recv()
         value = total[0, d] + b_in[0, d].astype(jnp.float32) + a_in[d].astype(jnp.float32)
@@ -385,9 +412,28 @@
         def _():
             total[0, d] = value
 
+    def stage(k, carry):
+        @pl.when(k < depth)
+        def _():
+            unit(3, slab(k))
+            unit(2, slab(k))
+
+        @pl.when(k > 0)
+        def _():
+            cross_a(slab(k - 1))
+
+        @pl.when(k < depth)
+        def _():
+            unit(1, slab(k))
+            unit(0, slab(k))
+
+        @pl.when(k > 0)
+        def _():
+            cross_z(slab(k - 1))
+
         return carry
 
-    lax.fori_loop(0, depth, cross_z, 0)
+    lax.fori_loop(0, depth + 1, stage, 0)
     value = total[0, 0]
     for d in range(1, depth):
         to_z(d).wait_recv()
@@ -448,7 +494,7 @@
             pltpu.VMEM((2, cols, slots + 1, side, side), bf16),
             pltpu.VMEM((2, cols // 2, 2 * rows, 2 * side), jnp.float32),
             dma((2,)),
-            dma((depth,)),
+            dma((2, depth)),
             dma((depth,)),
             dma((2, depth)),
             dma((4, depth)),

time: 146 us -> 135 us (0.925)
  the two profiles are of different devices: /device:TPU:9 before, /device:TPU:0 now
where the time goes in v2:
time: 135 us
  Pallas kernels  130 us (96%)
  local copies, waits for them, and re-layouts  3.03 us (2%)
  other arithmetic  1.65 us (1%)
    pallas_call x1, Pallas kernels, plane_body(): pl.pallas_call(functools.partial(in_kernel, depth), out_shape=jax.ShapeDt...  75.3 us
    pallas_call x1, Pallas kernels, plane_body(): pl.pallas_call(functools.partial(out_kernel, depth), out_shape=jax.ShapeD...  55 us

profile of v2, /device:TPU:0, one launch (start us, length us, event | category | flops | bytes accessed | tf_op | source)
XLA Modules:
  0.0 135.0 jit_solution(4405996275230402165)
XLA Ops:
  0.0 0.7 pad_add_fusion
  0.7 0.1 constant_dynamic-slice_fusion
  0.8 0.7 fusion.2
  1.5 0.1 copy.11
  1.6 0.2 select_reduce_fusion
  1.8 0.6 slice_bitcast_fusion.1.slot_of
  2.4 0.6 slice_bitcast_fusion.slot_of
  3.0 75.3 %shard_map.100.hidden = bf16[2,256,1024]{2,1,0:T(8,128)(2,1)} custom-call(s32[16,64]{1,0:T(8,128)} %slice_bitcast_fusion.slot_of, bf16[256,512]{1,0:T(8,128)(2,1)} %tokens.1, bf16[8,22,128,128]{3,2,1,0:T(8,128)(2,1)} %gate_hbm.1, bf16[8,22,128,128]{3,2,1,0:T(8,128)(2,1)} %up_hbm.1), custom_call_target="tpu_custom_call" | custom-call | tf_op jit(solution)/shard_map/pallas_call | solution.py:487
  78.3 55.0 %shard_map.101 = bf16[256,512]{1,0:T(8,128)(2,1)} custom-call(s32[8,64]{1,0:T(8,128)} %slice_bitcast_fusion.1.slot_of, bf16[2,256,1024]{2,1,0:T(8,128)(2,1)} %shard_map.100.hidden, bf16[8,22,128,128]{3,2,1,0:T(8,128)(2,1)} %down_hbm.1), custom_call_target="tpu_custom_call" | custom-call | tf_op jit(solution)/shard_map/pallas_call | solution.py:509
  133.3 1.7 %copy.13 = bf16[256,512]{1,0:T(8,128)(2,1)} copy(bf16[256,512]{1,0:T(8,128)(2,1)} %shard_map.101) | data formatting | bytes 524288
  (1 shorter events, 0.0 us)

commit v3 on v2

--- a/solution.py
+++ b/solution.py
@@ -8,7 +8,7 @@
 from jax.sharding import PartitionSpec as P
 
 MESH = pl.DeviceIdType.MESH
-VMEM_BYTES = 56 * 1024 * 1024
+VMEM_BYTES = 62 * 1024 * 1024
 
 
 def kept_mask(count_part, slot_num):
@@ -125,12 +125,12 @@
     )
 
 
-def in_kernel(
+def project_in(
+    place,
     depth,
     slot_of,
+    loads,
     tokens,
-    gate_hbm,
-    up_hbm,
     hidden,
     tok,
     weights,
@@ -143,25 +143,23 @@
     plane_recv,
     core_recv,
 ):
-    place = Place(depth)
-    cols, slots = gate_hbm.shape[0], gate_hbm.shape[1]
-    side = gate_hbm.shape[2]
-    rows = tokens.shape[0]
-    group = tokens.shape[1] // side
+    cols, slots, side = weights.shape[1], weights.shape[2] - 1, weights.shape[3]
+    rows, feats = tokens.shape
+    blocks = tok.shape[2] // side
     pairs = cols // 2
 
-    loads = [
-        pltpu.make_async_copy(src, weights.at[m, :, pl.ds(0, slots)], load_sem.at[m])
-        for m, src in enumerate((gate_hbm, up_hbm))
-    ]
-    for load in loads:
-        load.start()
-    tok[place.fs, place.x] = tokens[...]
+    def at(f, t):
+        row = pl.multiple_of(t * rows, rows)
+        col = pl.multiple_of((f % 4) * feats, feats)
+        return tok.at[f // 4, pl.ds(row, rows), pl.ds(col, feats)]
+
+    own = pltpu.make_async_copy(tokens, at(place.fs, place.x), load_sem.at[2])
+    own.start()
     greet(place)
+    own.wait()
 
     def shard(s, z, c):
-        f, t = place.spot(s, z, c)
-        return tok.at[f, t]
+        return at(*place.spot(s, z, c))
 
     def to_a(z):
         ref = shard(0, z, place.c)
@@ -206,40 +204,35 @@
     begin(place.z)
 
     weights[:, :, slots] = jnp.zeros((2, cols, side, side), weights.dtype)
+    take(1)
     acc[...] = jnp.zeros_like(acc)
     for load in loads:
         load.wait()
 
-    def multiply(z, dy, c):
-        f = (z * 2 + (place.y + dy) % 2) * 2 + c
-        left = tok[f].reshape(2 * rows, group * side)
-
-        def pair(n, carry):
-            for m in range(2):
-                panel = jnp.concatenate(
+    def multiply(z, n):
+        panel = jnp.concatenate(
+            [
+                jnp.concatenate(
                     [
-                        jnp.concatenate(
-                            [
-                                weights[m, 2 * n + e, slot_of[m * cols + 2 * n + e, f * group + i]]
-                                for e in range(2)
-                            ],
-                            axis=1,
-                        )
-                        for i in range(group)
+                        weights[m, 2 * n + e, slot_of[m * cols + 2 * n + e, z * blocks + i]]
+                        for m in range(2)
+                        for e in range(2)
                     ],
-                    axis=0,
+                    axis=1,
                 )
-                acc[m, n] += jnp.dot(left, panel, preferred_element_type=jnp.float32)
-            return carry
-
-        lax.fori_loop(0, pairs, pair, 0)
+                for i in range(blocks)
+            ],
+            axis=0,
+        )
+        acc[n] += jnp.dot(tok[z], panel, preferred_element_type=jnp.float32)
+
+    def multiply_some(z, part):
+        lax.fori_loop(
+            pairs * part // 3, pairs * (part + 1) // 3, lambda n, _: multiply(z, n), None
+        )
 
     def stage(j, carry):
         last = place.order(j - 1)
-
-        @pl.when(j + 1 < depth)
-        def _():
-            take(j + 1)
 
         @pl.when(j < depth)
         def _():
@@ -248,9 +241,15 @@
             to_b(1, z).start()
             to_core(1, z).start()
 
+        @pl.when(j + 2 < depth)
+        def _():
+            take(j + 2)
+
         @pl.when(j > 0)
         def _():
-            multiply(last, 0, place.c)
+            for s in range(4):
+                arrived_core(s, last)
+            multiply_some(last, 0)
 
         @pl.when(j < depth)
         def _():
@@ -260,7 +259,7 @@
 
         @pl.when(j > 0)
         def _():
-            multiply(last, 1, place.c)
+            multiply_some(last, 1)
 
         @pl.when(j < depth)
         def _():
@@ -270,20 +269,17 @@
 
         @pl.when(j > 0)
         def _():
-            for s in range(4):
-                arrived_core(s, last)
-            multiply(last, 0, 1 - place.c)
-            multiply(last, 1, 1 - place.c)
+            multiply_some(last, 2)
 
         return carry
 
     lax.fori_loop(0, depth + 1, stage, 0)
 
     for n in range(pairs):
-        gate = acc[0, n]
-        up = acc[1, n]
+        gate = acc[n, :, : 2 * side]
+        up = acc[n, :, 2 * side :]
         out = (gate / (1.0 + jnp.exp(-gate)) * up).astype(hidden.dtype)
-        hidden[:, :, n * 2 * side : (n + 1) * 2 * side] = out.reshape(2, rows, 2 * side)
+        hidden[:, n * 2 * side : (n + 1) * 2 * side] = out
 
     for z in range(depth):
         each_relay(z, lambda copy: copy.wait_send())
@@ -294,11 +290,11 @@
             to_core(s, z).wait_send()
 
 
-def out_kernel(
+def project_out(
+    place,
     depth,
     slot_of,
     hidden,
-    down_hbm,
     mixed,
     weights,
     total,
@@ -310,7 +306,6 @@
     a_in,
     z_out,
     z_in,
-    load_sem,
     c_send,
     c_recv,
     b_send,
@@ -320,33 +315,25 @@
     z_send,
     z_recv,
 ):
-    place = Place(depth)
-    cols, slots, side = down_hbm.shape[0], down_hbm.shape[1], down_hbm.shape[2]
+    cols, side = weights.shape[0], weights.shape[2]
+    rows = mixed.shape[0]
     group = mixed.shape[1] // side
-    pairs = group // 2
-
-    load = pltpu.make_async_copy(down_hbm, weights.at[:, pl.ds(0, slots)], load_sem)
-    load.start()
-    weights[:, slots] = jnp.zeros((cols, side, side), weights.dtype)
-    greet(place)
-    load.wait()
-
-    def share(f, t, store):
-        left = hidden[t]
-        for n in range(pairs):
-            panel = jnp.concatenate(
-                [
-                    jnp.concatenate(
-                        [weights[j, slot_of[j, f * group + 2 * n + e]] for e in range(2)], axis=1
-                    )
-                    for j in range(cols)
-                ],
-                axis=0,
-            )
-            store(
-                slice(n * 2 * side, (n + 1) * 2 * side),
-                jnp.dot(left, panel, preferred_element_type=jnp.float32),
-            )
+
+    def share(d, dy, c, store):
+        f = (place.ahead(d) * 2 + (place.y + dy) % 2) * 2 + c
+        panel = jnp.concatenate(
+            [
+                jnp.concatenate(
+                    [weights[j, slot_of[j, f * group + i]] for i in range(group)], axis=1
+                )
+                for j in range(cols)
+            ],
+            axis=0,
+        )
+        value = jnp.dot(hidden[...], panel, preferred_element_type=jnp.float32)
+        for t in range(2):
+            dx = (place.x + t) % 2
+            store(dy * (1 + c) + dx * (2 - c), value[t * rows : (t + 1) * rows])
 
     def to_core(s, d):
         return remote(
@@ -371,20 +358,20 @@
     def slab(k):
         return (k + 1) % depth
 
-    def unit(s, d):
-        f, t = place.spot(s, place.ahead(d), 1 - place.c)
-
-        def store_out(where, value):
-            core_out[s, d, :, where] = value.astype(core_out.dtype)
-
-        share(f, t, store_out)
-        to_core(s, d).start()
-        f, t = place.spot(s, place.ahead(d), place.c)
-
-        def store_own(where, value):
-            total[s, d, :, where] = value
-
-        share(f, t, store_own)
+    def other_share(d, dy):
+        def store(s, value):
+            core_out[s, d] = value.astype(core_out.dtype)
+            to_core(s, d).start()
+
+        share(d, dy, 1 - place.c, store)
+
+    def own_share(d, dy):
+        def store(s, value):
+            total[s, d] = value
+
+        share(d, dy, place.c, store)
+
+    def unite(s, d):
         to_core(s, d).wait_recv()
         value = total[s, d] + core_in[s, d].astype(jnp.float32)
         if s >= 2:
@@ -415,25 +402,35 @@
     def stage(k, carry):
         @pl.when(k < depth)
         def _():
-            unit(3, slab(k))
-            unit(2, slab(k))
-
-        @pl.when(k > 0)
+            d = slab(k)
+            other_share(d, 1)
+            own_share(d, 1)
+            unite(3, d)
+
+        @pl.when(k > 1)
+        def _():
+            cross_z(slab(k - 2))
+
+        @pl.when(k < depth)
+        def _():
+            d = slab(k)
+            other_share(d, 0)
+            own_share(d, 0)
+            unite(2, d)
+
+        @pl.when((k > 0) & (k < depth + 1))
         def _():
             cross_a(slab(k - 1))
 
         @pl.when(k < depth)
         def _():
-            unit(1, slab(k))
-            unit(0, slab(k))
-
-        @pl.when(k > 0)
-        def _():
-            cross_z(slab(k - 1))
+            d = slab(k)
+            unite(1, d)
+            unite(0, d)
 
         return carry
 
-    lax.fori_loop(0, depth + 1, stage, 0)
+    lax.fori_loop(0, depth + 2, stage, 0)
     value = total[0, 0]
     for d in range(1, depth):
         to_z(d).wait_recv()
@@ -448,6 +445,42 @@
             to_b(s, d).wait_send()
         for s in range(4):
             to_core(s, d).wait_send()
+
+
+def kernel(
+    depth,
+    in_num,
+    in_slots,
+    down_slots,
+    tokens,
+    gate_hbm,
+    up_hbm,
+    down_hbm,
+    mixed,
+    hidden,
+    in_weights,
+    down_weights,
+    down_sem,
+    *scratch,
+):
+    place = Place(depth)
+    cols, slots, side = down_hbm.shape[0], down_hbm.shape[1], down_hbm.shape[2]
+    load_sem = scratch[2]
+    loads = [
+        pltpu.make_async_copy(src, in_weights.at[m, :, pl.ds(0, slots)], load_sem.at[m])
+        for m, src in enumerate((gate_hbm, up_hbm))
+    ]
+    down_load = pltpu.make_async_copy(down_hbm, down_weights.at[:, pl.ds(0, slots)], down_sem)
+    for load in loads:
+        load.start()
+    down_load.start()
+    down_weights[:, slots] = jnp.zeros((cols, side, side), down_weights.dtype)
+    tok, acc = scratch[:2]
+    project_in(
+        place, depth, in_slots, loads, tokens, hidden, tok, in_weights, acc, *scratch[2:in_num]
+    )
+    down_load.wait()
+    project_out(place, depth, down_slots, hidden, mixed, down_weights, *scratch[in_num:])
 
 
 def plane_body(
@@ -484,63 +517,65 @@
     anywhere = pl.BlockSpec(memory_space=pl.ANY)
     dma = pltpu.SemaphoreType.DMA
 
-    hidden = pl.pallas_call(
-        functools.partial(in_kernel, depth),
-        out_shape=jax.ShapeDtypeStruct((2, rows, cols * side), bf16),
-        in_specs=[smem, vmem, anywhere, anywhere],
+    in_scratch = [
+        pltpu.VMEM((depth, 2 * rows, 4 * feats), bf16),
+        pltpu.VMEM((cols // 2, 2 * rows, 4 * side), jnp.float32),
+        dma((3,)),
+        dma((2, depth)),
+        dma((depth,)),
+        dma((2, depth)),
+        dma((4, depth)),
+        dma((4, depth)),
+        dma((4, depth)),
+    ]
+    out_scratch = [
+        pltpu.VMEM((4, depth, rows, feats), jnp.float32),
+        pltpu.VMEM((4, depth, rows, feats), bf16),
+        pltpu.VMEM((4, depth, rows, feats), bf16),
+        pltpu.VMEM((2, depth, rows, feats), bf16),
+        pltpu.VMEM((2, depth, rows, feats), bf16),
+        pltpu.VMEM((depth, rows, feats), bf16),
+        pltpu.VMEM((depth, rows, feats), bf16),
+        pltpu.VMEM((depth, rows, feats), bf16),
+        pltpu.VMEM((depth, rows, feats), bf16),
+        dma((4, depth)),
+        dma((4, depth)),
+        dma((2, depth)),
+        dma((2, depth)),
+        dma((depth,)),
+        dma((depth,)),
+        dma((depth,)),
+        dma((depth,)),
+    ]
+    return pl.pallas_call(
+        functools.partial(kernel, depth, len(in_scratch)),
+        out_shape=jax.ShapeDtypeStruct((rows, feats), bf16),
+        in_specs=[smem, smem, vmem, anywhere, anywhere, anywhere],
         out_specs=vmem,
         scratch_shapes=[
-            pltpu.VMEM((fsdp, 2, rows, feats), bf16),
+            pltpu.VMEM((2 * rows, cols * side), bf16),
             pltpu.VMEM((2, cols, slots + 1, side, side), bf16),
-            pltpu.VMEM((2, cols // 2, 2 * rows, 2 * side), jnp.float32),
-            dma((2,)),
-            dma((2, depth)),
-            dma((depth,)),
-            dma((2, depth)),
-            dma((4, depth)),
-            dma((4, depth)),
-            dma((4, depth)),
-        ],
+            pltpu.VMEM((cols, slots + 1, side, side), bf16),
+            dma(()),
+        ]
+        + in_scratch
+        + out_scratch,
         compiler_params=pltpu.CompilerParams(
             collective_id=0, has_side_effects=True, vmem_limit_bytes=VMEM_BYTES
         ),
-    )(slot_of[:2].reshape(2 * cols, row_blocks), tokens, gate_blocks, up_blocks)
-
-    return pl.pallas_call(
-        functools.partial(out_kernel, depth),
-        out_shape=jax.ShapeDtypeStruct((rows, feats), bf16),
-        in_specs=[smem, vmem, anywhere],
-        out_specs=vmem,
-        scratch_shapes=[
-            pltpu.VMEM((cols, slots + 1, side, side), bf16),
-            pltpu.VMEM((4, depth, rows, feats), jnp.float32),
-            pltpu.VMEM((4, depth, rows, feats), bf16),
-            pltpu.VMEM((4, depth, rows, feats), bf16),
-            pltpu.VMEM((2, depth, rows, feats), bf16),
-            pltpu.VMEM((2, depth, rows, feats), bf16),
-            pltpu.VMEM((depth, rows, feats), bf16),
-            pltpu.VMEM((depth, rows, feats), bf16),
-            pltpu.VMEM((depth, rows, feats), bf16),
-            pltpu.VMEM((depth, rows, feats), bf16),
-            dma(()),
-            dma((4, depth)),
-            dma((4, depth)),
-            dma((2, depth)),
-            dma((2, depth)),
-            dma((depth,)),
-            dma((depth,)),
-            dma((depth,)),
-            dma((depth,)),
-        ],
-        compiler_params=pltpu.CompilerParams(
-            collective_id=1, has_side_effects=True, vmem_limit_bytes=VMEM_BYTES
-        ),
-    )(slot_of[2], hidden, down_blocks)
+    )(
+        slot_of[:2].reshape(2 * cols, row_blocks),
+        slot_of[2],
+        tokens,
+        gate_blocks,
+        up_blocks,
+        down_blocks,
+    )
 
 
 def solution(mesh):
     fsdp, tp = mesh.shape["fsdp"], mesh.shape["tp"]
-    if tp == 2 and fsdp % 4 == 0:
+    if tp == 2 and fsdp % 4 == 0 and fsdp >= 8:
         body = functools.partial(plane_body, fsdp // 4)
     else:
         body = general_body

time: 135 us -> 110 us (0.81)
  Pallas kernels: 130 us -> 105 us
    pallas_call x2 -> x1, Pallas kernels: 130 us -> 105 us  [plane_body(): pl.pallas_call(functools.partial(kernel, depth, len(in_scratch)), out_sha...]
where the time goes in v3:
time: 110 us
  Pallas kernels  105 us (95%)
  local copies, waits for them, and re-layouts  3.03 us (3%)
  other arithmetic  1.65 us (2%)
    pallas_call x1, Pallas kernels, plane_body(): pl.pallas_call(functools.partial(kernel, depth, len(in_scratch)), out_sha...  105 us

profile of v3, /device:TPU:0, one launch (start us, length us, event | category | flops | bytes accessed | tf_op | source)
XLA Modules:
  0.0 109.6 jit_solution(7552923153962406411)
XLA Ops:
  0.0 0.7 pad_add_fusion
  0.7 0.1 constant_dynamic-slice_fusion
  0.8 0.7 fusion.2
  1.5 0.1 copy.11
  1.6 0.2 select_reduce_fusion
  1.8 0.6 slice_bitcast_fusion.1.down_slots
  2.4 0.6 slice_bitcast_fusion.in_slots
  3.0 104.9 %shard_map.100 = bf16[256,512]{1,0:T(8,128)(2,1)} custom-call(s32[16,64]{1,0:T(8,128)} %slice_bitcast_fusion.in_slots, s32[8,64]{1,0:T(8,128)} %slice_bitcast_fusion.1.down_slots, bf16[256,512]{1,0:T(8,128)(2,1)} %tokens.1, bf16[8,22,128,128]{3,2,1,0:T(8,128)(2,1)} %gate_hbm.1, bf16[8,22,128,128]{3,2,1,0:T(8,128)(2,1)} %up_hbm.1, ...), custom_call_target="tpu_custom_call" | custom-call | tf_op jit(solution)/shard_map/pallas_call | solution.py:550
  108.0 1.7 %copy.13 = bf16[256,512]{1,0:T(8,128)(2,1)} copy(bf16[256,512]{1,0:T(8,128)(2,1)} %shard_map.100) | data formatting | bytes 524288
  (1 shorter events, 0.0 us)

commit v4 on v3

--- a/solution.py
+++ b/solution.py
@@ -324,7 +324,7 @@
         panel = jnp.concatenate(
             [
                 jnp.concatenate(
-                    [weights[j, slot_of[j, f * group + i]] for i in range(group)], axis=1
+                    [weights[j, slot_of[2 * cols + j, f * group + i]] for i in range(group)], axis=1
                 )
                 for j in range(cols)
             ],
@@ -406,6 +406,7 @@
             other_share(d, 1)
             own_share(d, 1)
             unite(3, d)
+            pl.when(place.c == 1)(lambda: unite(2, d))
 
         @pl.when(k > 1)
         def _():
@@ -416,7 +417,7 @@
             d = slab(k)
             other_share(d, 0)
             own_share(d, 0)
-            unite(2, d)
+            pl.when(place.c == 0)(lambda: unite(2, d))
 
         @pl.when((k > 0) & (k < depth + 1))
         def _():
@@ -450,8 +451,7 @@
 def kernel(
     depth,
     in_num,
-    in_slots,
-    down_slots,
+    slot_of,
     tokens,
     gate_hbm,
     up_hbm,
@@ -477,10 +477,10 @@
     down_weights[:, slots] = jnp.zeros((cols, side, side), down_weights.dtype)
     tok, acc = scratch[:2]
     project_in(
-        place, depth, in_slots, loads, tokens, hidden, tok, in_weights, acc, *scratch[2:in_num]
+        place, depth, slot_of, loads, tokens, hidden, tok, in_weights, acc, *scratch[2:in_num]
     )
     down_load.wait()
-    project_out(place, depth, down_slots, hidden, mixed, down_weights, *scratch[in_num:])
+    project_out(place, depth, slot_of, hidden, mixed, down_weights, *scratch[in_num:])
 
 
 def plane_body(
@@ -550,7 +550,7 @@
     return pl.pallas_call(
         functools.partial(kernel, depth, len(in_scratch)),
         out_shape=jax.ShapeDtypeStruct((rows, feats), bf16),
-        in_specs=[smem, smem, vmem, anywhere, anywhere, anywhere],
+        in_specs=[smem, vmem, anywhere, anywhere, anywhere],
         out_specs=vmem,
         scratch_shapes=[
             pltpu.VMEM((2 * rows, cols * side), bf16),
@@ -564,8 +564,7 @@
             collective_id=0, has_side_effects=True, vmem_limit_bytes=VMEM_BYTES
         ),
     )(
-        slot_of[:2].reshape(2 * cols, row_blocks),
-        slot_of[2],
+        slot_of.reshape(3 * cols, row_blocks),
         tokens,
         gate_blocks,
         up_blocks,

time: 110 us -> 109 us (level)
  local copies, waits for them, and re-layouts: 3.03 us -> 1.84 us
where the time goes in v4:
time: 109 us; the launch traced here: 108 us
  Pallas kernels  104 us (95%)
  other arithmetic  2.26 us (2%)
  local copies, waits for them, and re-layouts  1.84 us (2%)
    pallas_call x1, Pallas kernels, plane_body(): pl.pallas_call(functools.partial(kernel, depth, len(in_scratch)), out_sha...  104 us

profile of v4, /device:TPU:0, one launch (start us, length us, event | category | flops | bytes accessed | tf_op | source)
XLA Modules:
  0.0 108.3 jit_solution(4993179355140996195)
XLA Ops:
  0.0 0.7 pad_add_fusion
  0.7 0.1 constant_dynamic-slice_fusion
  0.8 0.7 fusion.2
  1.5 0.1 copy.11
  1.6 0.8 select_reduce_fusion
  2.4 104.2 %shard_map.100 = bf16[256,512]{1,0:T(8,128)(2,1)} custom-call(s32[24,64]{1,0:T(8,128)} %bitcast.7, bf16[256,512]{1,0:T(8,128)(2,1)} %tokens.1, bf16[8,22,128,128]{3,2,1,0:T(8,128)(2,1)} %gate_hbm.1, bf16[8,22,128,128]{3,2,1,0:T(8,128)(2,1)} %up_hbm.1, bf16[8,22,128,128]{3,2,1,0:T(8,128)(2,1)} %down_hbm.1), custom_call_target="tpu_custom_call" | custom-call | tf_op jit(solution)/shard_map/pallas_call | solution.py:550
  106.6 1.7 %copy.13 = bf16[256,512]{1,0:T(8,128)(2,1)} copy(bf16[256,512]{1,0:T(8,128)(2,1)} %shard_map.100) | data formatting | bytes 524288
  (1 shorter events, 0.0 us)
